TPU v7x, 32 devices: a whole 2x2x4 slice. The times are simulated.
32 devices in a mesh: pairs: 8 (over z, y), cols: 4 (over x, core).
Axes of the slice: x: 2, y: 2, z: 4, core: 2. Of those that a mesh axis runs over, the one named last changes fastest.
Arguments:
- state: float32 [2, 64, 64, 16384], P(None, 'pairs', None, 'cols'), may hold values from -6 to 6
- sector_mix: float32 [127, 64, 64], P(None, None, 'cols'), may hold values from -2 to 2
- kerr_rates: float32 [2], replicated, may hold values from 0.002 to 0.02
- column_load: int32 [16384], P('cols'), may hold values from 0 to 255
Outputs:
- evolved: float32 [2, 64, 64, 16384], P(None, 'pairs', None, 'cols')
- moment: float32 [1], replicated
All inputs are finite; a program needn't handle non-finite values.
Results may differ from a plain program's by a relative error of at most 0.0003.
Values sent between devices are 32-bit elements; how exact they have to be, the bound alone decides.
A program may use at most 192 MiB of HBM per device.

v0:
```python
import jax
import jax.numpy as jnp
import numpy as np
from jax import lax
from jax.sharding import PartitionSpec as P

THIRD = 64
MEMB = 128
WINDOW = 2


def build_tables(levels, pair_count):
    members = [[g] for g in range(2 * levels)]
    per_device = len(members) // pair_count
    per_source = levels // pair_count
    row_count = per_source * levels
    layout_rows = per_device * levels
    mat_index = -np.ones((pair_count, per_device, levels, levels), np.int64)
    buckets = [[[] for owner_id in range(pair_count)] for source_id in range(pair_count)]
    for group_id in range(len(members)):
        owner = group_id // per_device
        local_group = group_id % per_device
        offset = 0
        for sector in members[group_id]:
            if sector > 2 * levels - 2:
                continue
            low_end = max(0, sector - levels + 1)
            high_end = min(sector, levels - 1)
            sector_size = high_end - low_end + 1
            span = np.arange(sector_size)
            mat_index[
                owner, local_group, offset : offset + sector_size, offset : offset + sector_size
            ] = (sector * levels * levels + span[:, None] * levels + span[None, :])
            for step in range(sector_size):
                photon_one = low_end + step
                photon_two = sector - photon_one
                source = photon_one // per_source
                local_row = (photon_one - source * per_source) * levels + photon_two
                position = local_group * levels + offset + step
                buckets[source][owner].append((position, local_row))
            offset += sector_size
    slot_count = max((len(entries) for bucket_row in buckets for entries in bucket_row))
    send_idx = np.zeros((pair_count, pair_count, slot_count), np.int32)
    layout_idx = np.zeros((pair_count, layout_rows), np.int32)
    back_idx = np.zeros((pair_count, pair_count, slot_count), np.int32)
    row_idx = np.zeros((pair_count, row_count), np.int32)
    for source in range(pair_count):
        for owner in range(pair_count):
            entries = sorted(buckets[source][owner])
            for slot, (position, local_row) in enumerate(entries):
                send_idx[source, owner, slot] = local_row
                layout_idx[owner, position] = source * slot_count + slot
                back_idx[owner, source, slot] = position
                row_idx[source, local_row] = owner * slot_count + slot
    return (send_idx, layout_idx, back_idx, row_idx, mat_index.astype(np.int32), slot_count)


def local(state, sector_mix, kerr_rates, column_load):
    full_mix = lax.all_gather(sector_mix, "cols", axis=2, tiled=True)
    pair_count = lax.axis_size("pairs")
    device = lax.axis_index("pairs")
    col_device = lax.axis_index("cols")
    local_one = state.shape[1]
    levels = state.shape[2]
    col_count = state.shape[3]
    row_count = local_one * levels
    tables = build_tables(levels, pair_count)
    send_idx, layout_idx, back_idx, row_idx, mat_index, slot_count = tables
    flat_state = state.reshape(2, row_count, col_count)
    send_rows = jnp.asarray(send_idx)[device].reshape(-1)
    outgoing = jnp.take(flat_state, send_rows, axis=1).reshape(2, pair_count, slot_count, col_count)
    my_layout = jnp.asarray(layout_idx)[device]
    my_back = jnp.asarray(back_idx)[device].reshape(-1)
    my_mat = jnp.asarray(mat_index)[device]
    flat_mix = full_mix.reshape(-1)
    blocks = jnp.where(
        my_mat >= 0, jnp.take(flat_mix, jnp.maximum(my_mat, 0)), jnp.zeros((), jnp.float32)
    )
    groups = my_mat.shape[0]
    arrived = lax.all_to_all(outgoing, "pairs", split_axis=1, concat_axis=1, tiled=True)
    item_count = arrived.shape[3]
    gathered = jnp.take(arrived.reshape(2, pair_count * slot_count, item_count), my_layout, axis=1)
    gathered = gathered.reshape(2, groups, levels, item_count)
    combined = jnp.einsum("gij,pgjc->pgic", blocks, gathered, precision=lax.Precision.HIGHEST)
    leaving = jnp.take(combined.reshape(2, groups * levels, item_count), my_back, axis=1)
    leaving = leaving.reshape(2, pair_count, slot_count, item_count)
    returned = lax.all_to_all(leaving, "pairs", split_axis=1, concat_axis=1, tiled=True)
    mixed_rows = jnp.take(
        returned.reshape(2, pair_count * slot_count, col_count),
        jnp.asarray(row_idx)[device],
        axis=1,
    )
    real_part = mixed_rows[0]
    imag_part = mixed_rows[1]
    row_ids = jnp.arange(row_count, dtype=jnp.int32)
    photon_one = (device * local_one + row_ids // levels).astype(jnp.float32)
    photon_two = (row_ids % levels).astype(jnp.float32)
    loads = column_load.astype(jnp.float32)
    phases = (kerr_rates[0] * photon_one + kerr_rates[1] * photon_two)[:, None] * loads[None, :]
    cosine = jnp.cos(phases)
    sine_part = jnp.sin(phases)
    evolved = jnp.stack(
        [cosine * real_part - sine_part * imag_part, sine_part * real_part + cosine * imag_part]
    )
    evolved = evolved.reshape(2, local_one, levels, col_count)
    col_ids = col_device * col_count + jnp.arange(col_count, dtype=jnp.int32)
    third_level = (col_ids // (MEMB * WINDOW)).astype(jnp.float32)
    weight = (photon_one + 1.0)[:, None] * (third_level + 1.0)[None, :]
    partial_term = jnp.sum(weight * (real_part * real_part + imag_part * imag_part))
    summed = lax.psum(partial_term, ("pairs", "cols"))
    moment = summed / float(levels * levels * col_count * lax.axis_size("cols") * levels * THIRD)
    return (evolved, moment.reshape(1))


def solution(mesh):
    placed = (P(None, "pairs", None, "cols"), P(None, None, "cols"), P(), P("cols"))
    return jax.shard_map(
        local,
        mesh=mesh,
        in_specs=placed,
        out_specs=(P(None, "pairs", None, "cols"), P()),
        check_vma=False,
    )
```

profile of v0, /device:TPU:9, one launch (start us, length us, event | category | flops | bytes accessed | tf_op | source)
XLA Modules:
  0.0 2108.6 jit_solution(12733668764925936796)
XLA Ops:
  8.6 28.7 %copy.19 = f32[2,8,64,4096]{3,0,2,1:T(2,128)} copy(f32[2,8,64,4096]{3,2,1,0:T(8,128)} %param.11) | data formatting | bytes 33554432 | tf_op args[0]
  37.2 69.3 %gather_fusion = f32[1024,2,4096]{2,1,0:T(2,128)} fusion(f32[2,512,4096]{2,0,1:T(2,128)} %bitcast.67, s32[1024]{0:T(1024)S(1)} %broadcast_clamp_fusion.1), kind=kCustom, calls=%fused_computation.2 | custom fusion | bytes 67112960 | tf_op jit(solution)/shard_map/jit(_take)/gather | solution.py:71
  106.5 28.8 %broadcast_select_fusion.2 = f32[2,8,128,4096]{3,0,2,1:T(2,128)} fusion(f32[2,8,128,4096]{3,0,2,1:T(2,128)} %bitcast.69, pred[8,128]{1,0:T(8,128)(4,1)S(1)} %compare_and_fusion.1), kind=kLoop, calls=%fused_computation.9 | loop fusion | flops 8388608 | bytes 67109888 | tf_op jit(solution)/shard_map/jit(_take)/select_n | solution.py:71
  135.3 7.1 all-to-all-start
  143.1 1.1 dynamic-slice_maximum_fusion
  144.4 1.3 fusion.36
  145.6 1.3 fusion.29
  146.9 0.8 constant_dynamic-slice_fusion
  148.9 20.1 all-gather.2.cloned.1.call-done
  169.0 5.6 copy.21
  174.6 3.2 reshape.277
  177.9 362.7 %gather_fusion.1 = f32[65536]{0:T(1024)S(1)} fusion(f32[520192]{0:T(1024)S(1)} %reshape.277, s32[65536]{0:T(1024)S(1)} %broadcast_clamp_fusion), kind=kCustom, calls=%fused_computation.3 | custom fusion | bytes 786432 | tf_op jit(solution)/shard_map/jit(_take)/gather | solution.py:77
  540.7 322.4 %all-to-all-done = f32[2,8,128,4096]{3,0,2,1:T(2,128)} async-done(((f32[2,8,128,4096]{3,0,2,1:T(2,128)}), f32[2,8,128,4096]{3,0,2,1:T(2,128)}, u32[]{:S(2)}, u32[]{:S(2)}) %all-to-all-start) | async-done | bytes 33554464 | tf_op jit(solution)/shard_map/all_to_all | solution.py:80
  863.2 79.6 %gather_fusion.3 = f32[1024,2,4096]{2,1,0:T(2,128)} fusion(f32[2,1024,4096]{2,0,1:T(2,128)} %bitcast.11, s32[1024]{0:T(1024)S(1)} %copy-done.2), kind=kCustom, calls=%fused_computation.clone | custom fusion | bytes 67112960 | tf_op jit(solution)/shard_map/jit(_take)/gather | solution.py:82
  942.8 29.5 %broadcast_select_fusion.1 = f32[1024,2,4096]{2,1,0:T(2,128)} fusion(f32[1024,2,4096]{2,1,0:T(2,128)} %gather_fusion.3, pred[1024]{0:T(1024)(128)(4,1)S(1)} %copy-done.4), kind=kLoop, calls=%fused_computation.8 | loop fusion | flops 8388608 | bytes 67109888 | tf_op jit(solution)/shard_map/jit(_take)/select_n | solution.py:82
  972.3 51.7 %fusion.3 = f32[2,16,64,4096]{3,2,0,1:T(8,128)} fusion(f32[2,16,64,4096]{3,0,2,1:T(2,128)} %bitcast.66, f32[16,64,64]{2,1,0:T(8,128)S(1)} %reshape.307, s32[8,16,64,64]{3,2,1,0:T(8,128)} %constant.135.clone, s32[]{:T(128)S(6)} %select_n.99), kind=kOutput, calls=%fused_computation.13 | convolution fusion | flops 6442778624 | bytes 67895296 | tf_op jit(solution)/shard_map/gij,pgjc->pgic/dot_general | solution.py:84
  1024.0 22.9 %copy.23 = f32[2,16,64,4096]{3,2,1,0:T(8,128)} copy(f32[2,16,64,4096]{3,2,0,1:T(8,128)} %fusion.3) | data formatting | bytes 67108864 | tf_op jit(solution)/shard_map/gij,pgjc->pgic/transpose | solution.py:84
  1046.9 55.3 %copy.24 = f32[2,1024,4096]{2,0,1:T(2,128)} copy(f32[2,1024,4096]{2,1,0:T(8,128)} %bitcast.70) | data formatting | bytes 67108864 | tf_op jit(solution)/shard_map/reshape | solution.py:85
  1102.2 76.7 %gather_fusion.4 = f32[1024,2,4096]{2,1,0:T(2,128)} fusion(f32[2,1024,4096]{2,0,1:T(2,128)} %copy.24, s32[1024]{0:T(1024)S(1)} %copy-done.1), kind=kCustom, calls=%fused_computation.1.clone | custom fusion | bytes 67112960 | tf_op jit(solution)/shard_map/jit(_take)/gather | solution.py:85
  1178.9 29.5 %broadcast_select_fusion = f32[1024,2,4096]{2,1,0:T(2,128)} fusion(f32[1024,2,4096]{2,1,0:T(2,128)} %gather_fusion.4, pred[1024]{0:T(1024)(128)(4,1)S(1)} %copy-done.5), kind=kLoop, calls=%fused_computation.7 | loop fusion | flops 8388608 | bytes 67109888 | tf_op jit(solution)/shard_map/jit(_take)/select_n | solution.py:85
  1208.4 38.3 %all-to-all-start.1 = ((f32[2,8,128,4096]{3,0,2,1:T(2,128)}), f32[2,8,128,4096]{3,0,2,1:T(2,128)}, u32[]{:S(2)}, u32[]{:S(2)}) async-start(f32[2,8,128,4096]{3,0,2,1:T(2,128)} %bitcast.68), calls=%async_computation.1 | async-start | bytes 67108864 | tf_op jit(solution)/shard_map/all_to_all | solution.py:87
  1246.6 0.7 compare_select_fusion.1
  1247.4 0.7 constant_dynamic-slice_fusion.2
  1248.7 1.3 fusion.42
  1250.0 717.3 %all-to-all-done.1 = f32[2,8,128,4096]{3,0,2,1:T(2,128)} async-done(((f32[2,8,128,4096]{3,0,2,1:T(2,128)}), f32[2,8,128,4096]{3,0,2,1:T(2,128)}, u32[]{:S(2)}, u32[]{:S(2)}) %all-to-all-start.1) | async-done | bytes 33554464 | tf_op jit(solution)/shard_map/all_to_all | solution.py:87
  1967.3 27.7 %gather_fusion.2 = f32[512,2,4096]{2,1,0:T(2,128)} fusion(f32[2,1024,4096]{2,0,1:T(2,128)} %bitcast.22, s32[1024]{0:T(1024)S(1)} %pad_clamp_fusion), kind=kCustom, calls=%fused_computation.4 | custom fusion | bytes 33556480 | tf_op jit(solution)/shard_map/jit(_take)/gather | solution.py:88
  1995.1 15.4 fusion.2
  2010.5 6.2 copy-done
  2016.7 3.0 fusion.12
  2019.7 40.2 %psum.7 = f32[]{:T(128)} all-reduce(f32[]{:T(128)} %fusion.12), channel_id=1, replica_groups=mesh['pairs'=8,'cols'=4] {'pairs','cols'}, use_global_device_ids=true, to_apply=%region_1.3 | all-reduce | flops 1 | bytes 8 | tf_op jit(solution)/shard_map/psum | solution.py:110
  2059.9 33.3 %fusion.10 = (f32[1,512,4096]{2,1,0:T(8,128)S(1)}, f32[1,512,4096]{2,1,0:T(8,128)S(1)}) fusion(f32[2,512,4096]{2,1,0:T(8,128)} %copy-done, f32[4096]{0:T(1024)S(1)} %convert_element_type.29, f32[512]{0:T(512)S(1)} %fusion.42), kind=kLoop, calls=%fused_computation.20 | loop fusion | flops 14680064 | bytes 33572864 | tf_op jit(solution)/shard_map/sub | solution.py:103
  2093.2 6.4 pad_maximum_fusion
  (30 shorter events, 4.3 us)
Async XLA Ops:
  135.3 727.9 %all-to-all-start = ((f32[2,8,128,4096]{3,0,2,1:T(2,128)}), f32[2,8,128,4096]{3,0,2,1:T(2,128)}, u32[]{:S(2)}, u32[]{:S(2)}) async-start(f32[2,8,128,4096]{3,0,2,1:T(2,128)} %broadcast_select_fusion.2), calls=%async_computation | async-start | bytes 67108864 | tf_op jit(solution)/shard_map/all_to_all | solution.py:80
  142.4 26.7 %all-gather.2.cloned.1.call-start = ((), (), s32[]{:S(2)}) async-start(), calls=%async_computation.2 | async-start | bytes 2621440 | tf_op jit(solution)/shard_map/all_gather | solution.py:59
  177.9 685.3 %copy-start.2 = (s32[1024]{0:T(1024)S(1)}, s32[1024]{0:T(1024)}, u32[]{:S(2)}) copy-start(s32[1024]{0:T(1024)} %fusion.37) | copy-start | bytes 12292
  863.2 79.6 %copy-start.4 = (pred[1024]{0:T(1024)(128)(4,1)S(1)}, pred[1024]{0:T(1024)(128)(4,1)}, u32[]{:S(2)}) copy-start(pred[1024]{0:T(1024)(128)(4,1)} %compare_and_fusion) | copy-start | bytes 3076
  1046.9 55.3 %copy-start.1 = (s32[1024]{0:T(1024)S(1)}, s32[1024]{0:T(1024)}, u32[]{:S(2)}) copy-start(s32[1024]{0:T(1024)} %fusion.29) | copy-start | bytes 12292
  1102.2 76.7 %copy-start.5 = (pred[1024]{0:T(1024)(128)(4,1)S(1)}, pred[1024]{0:T(1024)(128)(4,1)}, u32[]{:S(2)}) copy-start(pred[1024]{0:T(1024)(128)(4,1)} %fusion.36) | copy-start | bytes 3076
  1208.4 39.7 %copy-start.6 = (f32[2]{0:T(128)S(1)}, f32[2]{0:T(128)}, u32[]{:S(2)}) copy-start(f32[2]{0:T(128)} %param.13) | copy-start | bytes 28
  1208.4 758.9 %all-to-all-start.1 = ((f32[2,8,128,4096]{3,0,2,1:T(2,128)}), f32[2,8,128,4096]{3,0,2,1:T(2,128)}, u32[]{:S(2)}, u32[]{:S(2)}) async-start(f32[2,8,128,4096]{3,0,2,1:T(2,128)} %bitcast.68), calls=%async_computation.1 | async-start | bytes 67108864 | tf_op jit(solution)/shard_map/all_to_all | solution.py:87
  2010.5 6.2 copy-start
  2016.7 3.0 copy-start.3
Sparse Core Ops, SparseCore 0:
  144.8 24.2 all-gather.1
where the time goes:
time: 2120 us; the launch traced here: 2110 us
  waiting for transfers between devices  1060 us (50%)
  local copies, waits for them, and re-layouts  741 us (35%)
  other arithmetic  154 us (7%)
  matrix products  51.7 us (2%)
  starting transfers between devices  45.5 us (2%)
  blocking collectives  40.2 us (2%)
    all_to_all x1, waiting for transfers between devices, local(): lax.all_to_all(leaving, 'pairs', split_axis=1, concat_axis=1, tiled=True)  717 us
    gather x2, local copies, waits for them, and re-layouts, local(): jnp.take(flat_mix, jnp.maximum(my_mat, 0))  363 us
    all_to_all x1, waiting for transfers between devices, local(): lax.all_to_all(outgoing, 'pairs', split_axis=1, concat_axis=1, tiled=True)  322 us
    gather x1, local copies, waits for them, and re-layouts, local(): jnp.take(arrived.reshape(2, pair_count * slot_count, item_count), my_layo...  79.6 us
    gather x1, local copies, waits for them, and re-layouts, local(): jnp.take(combined.reshape(2, groups * levels, item_count), my_back, axis=1)  76.7 us
    gather x1, local copies, waits for them, and re-layouts, local(): jnp.take(flat_state, send_rows, axis=1)  69.3 us
    reshape x1, local copies, waits for them, and re-layouts, local(): combined.reshape(2, groups * levels, item_count)  55.3 us
    dot_general x1, matrix products, local(): jnp.einsum('gij,pgjc->pgic', blocks, gathered, precision=lax.Precision.HI...  51.7 us
  transfers between devices with their start and end apart: 3, of which 3 were waited for; matrix products, arithmetic and copies ran while one was open for 18% of the time, Pallas kernels for 0%

commit v1 on v0

v1 whole, which is shorter than its diff:
```python
import functools

import jax
import jax.numpy as jnp
from jax import lax
from jax.experimental import pallas as pl
from jax.experimental.pallas import tpu as pltpu
from jax.sharding import PartitionSpec as P

THIRD = 64
MEMB = 128
WINDOW = 2
BAND = 8
LANES = 128
PAD = 8
MESH = pl.DeviceIdType.MESH


def needed(group, p, q, local_one, levels):
    low = p * local_one + q * BAND
    high = low + local_one - 1 + BAND - 1
    return jnp.logical_or(
        jnp.logical_and(group == 0, low <= levels - 1),
        jnp.logical_and(group == 1, high >= levels),
    )


def enter(me, mine, count):
    barrier = pltpu.get_barrier_semaphore()

    def greet(k, carry):
        pl.semaphore_signal(
            barrier, inc=1, device_id=(lax.rem(me + k, count), mine), device_id_type=MESH
        )
        return carry

    lax.fori_loop(1, count, greet, 0)
    pl.semaphore_wait(barrier, count - 1)


def scatter_kernel(count, levels, state_ref, rows_ref, send_sem, recv_sem, own_sem):
    me = lax.axis_index("pairs")
    mine = lax.axis_index("cols")
    local_one = state_ref.shape[1]
    half = count // 2
    width = state_ref.shape[3] // half
    bands = levels // BAND
    enter(me, mine, count)

    def view(dest, q):
        start = pl.multiple_of(lax.rem(dest, half) * width, LANES)
        return state_ref.at[:, :, pl.ds(pl.multiple_of(q * BAND, BAND), BAND), pl.ds(start, width)]

    def place(source, q):
        return rows_ref.at[
            :, pl.ds(source * local_one, local_one), pl.ds(pl.multiple_of(q * BAND, BAND), BAND), :
        ]

    def remote(source, dest, q):
        return pltpu.make_async_remote_copy(
            src_ref=view(dest, q),
            dst_ref=place(source, q),
            send_sem=send_sem.at[dest, q],
            recv_sem=recv_sem.at[source, q],
            device_id=(dest, mine),
            device_id_type=MESH,
        )

    def own(q):
        return pltpu.make_async_copy(view(me, q), place(me, q), own_sem.at[q])

    def each(act):
        def outer(q, carry):
            def inner(k, carry):
                act(q, k)
                return carry

            return lax.fori_loop(1, count, inner, carry)

        lax.fori_loop(0, bands, outer, 0)

    def send(q, k):
        dest = lax.rem(me + k, count)

        @pl.when(needed(dest // half, me, q, local_one, levels))
        def _():
            remote(me, dest, q).start()

    def finish(q, k):
        dest = lax.rem(me + k, count)
        source = lax.rem(me + count - k, count)

        @pl.when(needed(dest // half, me, q, local_one, levels))
        def _():
            remote(me, dest, q).wait_send()

        @pl.when(needed(me // half, source, q, local_one, levels))
        def _():
            remote(source, me, q).wait_recv()

    def own_start(q, carry):
        @pl.when(needed(me // half, me, q, local_one, levels))
        def _():
            own(q).start()

        return carry

    def own_wait(q, carry):
        @pl.when(needed(me // half, me, q, local_one, levels))
        def _():
            own(q).wait()

        return carry

    each(send)
    lax.fori_loop(0, bands, own_start, 0)
    each(finish)
    lax.fori_loop(0, bands, own_wait, 0)


def return_kernel(count, levels, rows_ref, home_ref, send_sem, recv_sem, own_sem):
    me = lax.axis_index("pairs")
    mine = lax.axis_index("cols")
    local_one = home_ref.shape[2]
    half = count // 2
    width = rows_ref.shape[3]
    bands = levels // BAND
    enter(me, mine, count)

    def view(dest, q):
        return rows_ref.at[
            :, pl.ds(dest * local_one, local_one), pl.ds(pl.multiple_of(q * BAND, BAND), BAND), :
        ]

    def place(source, q):
        start = pl.multiple_of(lax.rem(source, half) * width, LANES)
        return home_ref.at[
            source // half, :, :, pl.ds(pl.multiple_of(q * BAND, BAND), BAND), pl.ds(start, width)
        ]

    def remote(source, dest, q):
        return pltpu.make_async_remote_copy(
            src_ref=view(dest, q),
            dst_ref=place(source, q),
            send_sem=send_sem.at[dest, q],
            recv_sem=recv_sem.at[source, q],
            device_id=(dest, mine),
            device_id_type=MESH,
        )

    def own(q):
        return pltpu.make_async_copy(view(me, q), place(me, q), own_sem.at[q])

    def each(act):
        def outer(q, carry):
            def inner(k, carry):
                act(q, k)
                return carry

            return lax.fori_loop(1, count, inner, carry)

        lax.fori_loop(0, bands, outer, 0)

    def send(q, k):
        dest = lax.rem(me + k, count)

        @pl.when(needed(me // half, dest, q, local_one, levels))
        def _():
            remote(me, dest, q).start()

    def finish(q, k):
        dest = lax.rem(me + k, count)
        source = lax.rem(me + count - k, count)

        @pl.when(needed(me // half, dest, q, local_one, levels))
        def _():
            remote(me, dest, q).wait_send()

        @pl.when(needed(source // half, me, q, local_one, levels))
        def _():
            remote(source, me, q).wait_recv()

    def own_start(q, carry):
        @pl.when(needed(me // half, me, q, local_one, levels))
        def _():
            own(q).start()

        return carry

    def own_wait(q, carry):
        @pl.when(needed(me // half, me, q, local_one, levels))
        def _():
            own(q).wait()

        return carry

    each(send)
    lax.fori_loop(0, bands, own_start, 0)
    each(finish)
    lax.fori_loop(0, bands, own_wait, 0)


def mix_kernel(levels, group_ref, mix_ref, rows_ref, mixed_ref, moment_ref, planes, factors):
    group = group_ref[0]
    bands = levels // BAND

    @pl.when(pl.program_id(0) == 0)
    def _():
        planes[...] = jnp.zeros_like(planes)

        def split(t, carry):
            whole = mix_ref[t]
            high = whole.astype(jnp.bfloat16)
            low = (whole - high.astype(jnp.float32)).astype(jnp.bfloat16)
            factors[t] = jnp.concatenate([high, high, low], axis=1)
            return carry

        lax.fori_loop(0, levels, split, 0)

    def move(act, which, stride):
        def level(n1, carry):
            for q in range(bands):
                plane = n1 + q * BAND - which * levels
                position = n1 if which == 0 else levels - 1 - q * BAND

                @pl.when(jnp.logical_and(plane > -BAND, plane < levels))
                def _():
                    start = (plane + PAD) * levels + position
                    for part in range(2):
                        act(part, n1, q, pl.ds(start, BAND, stride=stride))

            return carry

        lax.fori_loop(0, levels, level, 0)

    def put(part, n1, q, where):
        planes[part, where, :] = rows_ref[part, n1, q * BAND : (q + 1) * BAND, :]

    def get(part, n1, q, where):
        mixed_ref[part, n1, q * BAND : (q + 1) * BAND, :] = planes[part, where, :]

    def both(act):
        @pl.when(group == 0)
        def _():
            move(act, 0, levels)

        @pl.when(group == 1)
        def _():
            move(act, 1, levels - 1)

    both(put)
    row_ids = lax.broadcasted_iota(jnp.int32, (levels, 2 * LANES), 0)

    def sector(t, total):
        start = pl.multiple_of((t + PAD) * levels, BAND)
        block = jnp.concatenate(
            [planes[0, pl.ds(start, levels), :], planes[1, pl.ds(start, levels), :]], axis=1
        )
        high = block.astype(jnp.bfloat16)
        low = (block - high.astype(jnp.float32)).astype(jnp.bfloat16)
        found = jnp.dot(
            factors[t],
            jnp.concatenate([high, low, high], axis=0),
            preferred_element_type=jnp.float32,
        )
        size = jnp.where(group == 0, t + 1, levels - 1 - t)
        first = jnp.where(group == 0, 0, t + 1)
        found = jnp.where(row_ids < size, found, 0.0)
        planes[0, pl.ds(start, levels), :] = found[:, :LANES]
        planes[1, pl.ds(start, levels), :] = found[:, LANES:]
        weight = (row_ids + (first + 1)).astype(jnp.float32)
        term = weight * found * found
        for band in range(bands):
            total = total + term[band * BAND : (band + 1) * BAND]
        return total

    total = lax.fori_loop(
        0, levels, sector, jnp.zeros((BAND, 2 * LANES), jnp.float32), unroll=4
    )
    moment_ref[...] = total[:, :LANES] + total[:, LANES:]
    both(get)


def evolve_kernel(levels, offset_ref, one_ref, two_ref, home_ref, evolved_ref):
    offset = offset_ref[0]
    local_one = home_ref.shape[2]
    shape = home_ref.shape[3:]
    n2 = lax.broadcasted_iota(jnp.int32, shape, 0)
    cos_two, sin_two = two_ref[0], two_ref[1]
    for i in range(local_one):
        lower = n2 + (offset + i) < levels
        real = jnp.where(lower, home_ref[0, 0, i], home_ref[1, 0, i])
        imag = jnp.where(lower, home_ref[0, 1, i], home_ref[1, 1, i])
        cos_one, sin_one = one_ref[0, i : i + 1, :], one_ref[1, i : i + 1, :]
        cosine = cos_one * cos_two - sin_one * sin_two
        sine = sin_one * cos_two + cos_one * sin_two
        evolved_ref[0, i] = cosine * real - sine * imag
        evolved_ref[1, i] = sine * real + cosine * imag


def local(state, sector_mix, kerr_rates, column_load):
    full_mix = lax.all_gather(sector_mix, "cols", axis=2, tiled=True)
    count = lax.axis_size("pairs")
    me = lax.axis_index("pairs")
    mine = lax.axis_index("cols")
    _, local_one, levels, columns = state.shape
    half = count // 2
    width = columns // half
    bands = levels // BAND
    group = me // half
    f32 = jnp.float32
    semaphores = [
        pltpu.SemaphoreType.DMA((count, bands)),
        pltpu.SemaphoreType.DMA((count, bands)),
        pltpu.SemaphoreType.DMA((bands,)),
    ]
    anywhere = pl.BlockSpec(memory_space=pl.ANY)

    rows = pl.pallas_call(
        functools.partial(scatter_kernel, count, levels),
        out_shape=jax.ShapeDtypeStruct((2, levels, levels, width), f32),
        in_specs=[anywhere],
        out_specs=anywhere,
        scratch_shapes=semaphores,
        compiler_params=pltpu.CompilerParams(
            collective_id=0, has_side_effects=True, vmem_limit_bytes=56 << 20
        ),
        name="scatter",
    )(state)

    padded = jnp.pad(full_mix, ((0, 2 * levels - full_mix.shape[0]), (0, 0), (0, 0)))
    group_mix = lax.dynamic_slice(padded, (group * levels, 0, 0), (levels, levels, levels))
    mixed, moments = pl.pallas_call(
        functools.partial(mix_kernel, levels),
        grid=(width // LANES,),
        out_shape=(
            jax.ShapeDtypeStruct((2, levels, levels, width), f32),
            jax.ShapeDtypeStruct((BAND, width), f32),
        ),
        in_specs=[
            pl.BlockSpec(memory_space=pltpu.SMEM),
            pl.BlockSpec((levels, levels, levels), lambda c: (0, 0, 0)),
            pl.BlockSpec((2, levels, levels, LANES), lambda c: (0, 0, 0, c)),
        ],
        out_specs=(
            pl.BlockSpec((2, levels, levels, LANES), lambda c: (0, 0, 0, c)),
            pl.BlockSpec((BAND, LANES), lambda c: (0, c)),
        ),
        scratch_shapes=[
            pltpu.VMEM((2, (levels + 2 * PAD) * levels, LANES), f32),
            pltpu.VMEM((levels, levels, 3 * levels), jnp.bfloat16),
        ],
        compiler_params=pltpu.CompilerParams(vmem_limit_bytes=48 << 20),
        name="mix",
    )(group.reshape(1).astype(jnp.int32), group_mix, rows)

    first_column = mine * columns + lax.rem(me, half) * width
    column_ids = first_column + jnp.arange(width, dtype=jnp.int32)
    third_level = (column_ids // (MEMB * WINDOW)).astype(f32)
    partial_term = jnp.sum(moments * (third_level + 1.0)[None, :])
    summed = lax.psum(partial_term, ("pairs", "cols"))
    moment = summed / float(levels * levels * columns * lax.axis_size("cols") * levels * THIRD)

    home = pl.pallas_call(
        functools.partial(return_kernel, count, levels),
        out_shape=jax.ShapeDtypeStruct((2, 2, local_one, levels, columns), f32),
        in_specs=[anywhere],
        out_specs=anywhere,
        scratch_shapes=semaphores,
        compiler_params=pltpu.CompilerParams(
            collective_id=1, has_side_effects=True, vmem_limit_bytes=56 << 20
        ),
        name="give_back",
    )(mixed)

    loads = column_load.astype(f32)
    offset = me * local_one
    levels_one = (offset + jnp.arange(local_one)).astype(f32)
    levels_two = jnp.arange(levels).astype(f32)
    phase_one = (kerr_rates[0] * levels_one)[:, None] * loads[None, :]
    phase_two = (kerr_rates[1] * levels_two)[:, None] * loads[None, :]
    one = jnp.stack([jnp.cos(phase_one), jnp.sin(phase_one)])
    two = jnp.stack([jnp.cos(phase_two), jnp.sin(phase_two)])
    tile = min(columns, 512)
    evolved = pl.pallas_call(
        functools.partial(evolve_kernel, levels),
        grid=(columns // tile,),
        out_shape=jax.ShapeDtypeStruct((2, local_one, levels, columns), f32),
        in_specs=[
            pl.BlockSpec(memory_space=pltpu.SMEM),
            pl.BlockSpec((2, local_one, tile), lambda c: (0, 0, c)),
            pl.BlockSpec((2, levels, tile), lambda c: (0, 0, c)),
            pl.BlockSpec((2, 2, local_one, levels, tile), lambda c: (0, 0, 0, 0, c)),
        ],
        out_specs=pl.BlockSpec((2, local_one, levels, tile), lambda c: (0, 0, 0, c)),
        compiler_params=pltpu.CompilerParams(vmem_limit_bytes=48 << 20),
        name="evolve",
    )(offset.reshape(1).astype(jnp.int32), one, two, home)
    return (evolved, moment.reshape(1))


def solution(mesh):
    placed = (P(None, "pairs", None, "cols"), P(None, None, "cols"), P(), P("cols"))
    return jax.shard_map(
        local,
        mesh=mesh,
        in_specs=placed,
        out_specs=(P(None, "pairs", None, "cols"), P()),
        check_vma=False,
    )
```

time: 2120 us -> 774 us (0.37)
  waiting for transfers between devices: 1060 us -> 0.04 us
  local copies, waits for them, and re-layouts: 741 us -> 10.1 us
  Pallas kernels: 0 us -> 700 us
  other arithmetic: 154 us -> 6.32 us
  matrix products: 51.7 us -> 0 us
  starting transfers between devices: 45.5 us -> 0.04 us
    all_to_all x2 -> x0, waiting for transfers between devices: 1040 us -> none  [the longest x1 717 us: local(): lax.all_to_all(leaving, 'pairs', split_axis=1, concat_axis=1, tiled=True)]
    pallas_call x0 -> x4, Pallas kernels: none -> 700 us  [the longest x1 289 us: local(): pl.pallas_call(functools.partial(return_kernel, count, levels), out_shape...]
    gather x6 -> x0, local copies, waits for them, and re-layouts: 616 us -> none  [the longest x2 363 us: local(): jnp.take(flat_mix, jnp.maximum(my_mat, 0))]
    select_n x6 -> x0, other arithmetic: 104 us -> none  [the longest x1 29.5 us: local(): jnp.take(arrived.reshape(2, pair_count * slot_count, item_count), my_layo...]
    reshape x2 -> x0, local copies, waits for them, and re-layouts: 58.5 us -> none  [the longest x1 55.3 us: local(): combined.reshape(2, groups * levels, item_count)]
    dot_general x1 -> x0, matrix products: 51.7 us -> none  [local(): jnp.einsum('gij,pgjc->pgic', blocks, gathered, precision=lax.Precision.HI...]
    all_to_all x2 -> x0, starting transfers between devices: 45.3 us -> none  [the longest x1 38.3 us: local(): lax.all_to_all(leaving, 'pairs', split_axis=1, concat_axis=1, tiled=True)]
    sub x1 -> x0, other arithmetic: 33.3 us -> none  [local(): cosine * real_part - sine_part * imag_part]
  transfers between devices with their start and end apart: 3 -> 1, of which waited for: 3 -> 0; matrix products, arithmetic and copies ran while one was open for 18% -> 1% of each run, Pallas kernels for 0% -> 36%
where the time goes in v1:
time: 774 us; the launch traced here: 770 us
  Pallas kernels  700 us (90%)
  blocking collectives  37.9 us (5%)
  between operations  15.9 us (2%)
  local copies, waits for them, and re-layouts  10.1 us (1%)
    pallas_call x1, Pallas kernels, local(): pl.pallas_call(functools.partial(return_kernel, count, levels), out_shape...  289 us
    pallas_call x1, Pallas kernels, local(): pl.pallas_call(functools.partial(scatter_kernel, count, levels), out_shap...  277 us
    pallas_call x1, Pallas kernels, local(): pl.pallas_call(functools.partial(mix_kernel, levels), grid=(width // LANE...  116 us
    psum x1, blocking collectives, local(): summed = lax.psum(partial_term, ('pairs', 'cols'))  37.9 us
    pallas_call x1, Pallas kernels, local(): pl.pallas_call(functools.partial(evolve_kernel, levels), grid=(columns //...  18.5 us
  transfers between devices with their start and end apart: 1, of which 0 were waited for; matrix products, arithmetic and copies ran while one was open for 1% of the time, Pallas kernels for 36%

profile of v1, /device:TPU:9, one launch (start us, length us, event | category | flops | bytes accessed | tf_op | source)
XLA Modules:
  0.0 770.2 jit_solution(14928629517196682794)
XLA Ops:
  7.2 0.0 all-gather.2.cloned.1.call-start
  7.2 2.0 copy.7
  9.2 0.0 all-gather.2.cloned.1.call-update
  9.3 0.0 copy-start.1
  9.3 0.0 copy-start
  9.3 276.7 %scatter.1.rows_ref = f32[2,64,64,1024]{3,2,1,0:T(8,128)} custom-call(f32[2,8,64,4096]{3,2,1,0:T(8,128)} %state_ref.1), custom_call_target="tpu_custom_call" | custom-call | tf_op jit(solution)/shard_map/scatter/pallas_call | solution.py:319
  286.0 0.0 copy-done.1
  286.0 0.6 fusion.5
  286.6 0.0 copy-done
  286.6 0.6 convert_multiply_fusion
  287.3 0.6 convert_multiply_fusion.1
  287.9 0.5 multiply_cosine_fusion.1
  288.5 3.7 multiply_cosine_fusion
  292.2 0.2 pad_maximum_fusion.two_ref
  292.4 0.0 all-gather.2.cloned.1.call-done
  292.4 5.7 copy.8
  298.0 1.9 pad_dynamic-slice_fusion.mix_ref
  299.9 115.6 %mix.1 = (f32[2,64,64,1024]{3,2,1,0:T(8,128)}, f32[8,1024]{1,0:T(8,128)S(1)}) custom-call(s32[1]{0:T(128)} %bitcast.3.group_ref, f32[64,64,64]{2,1,0:T(8,128)S(1)} %pad_dynamic-slice_fusion.mix_ref, f32[2,64,64,1024]{3,2,1,0:T(8,128)} %scatter.1.rows_ref), custom_call_target="tpu_custom_call" | custom-call | tf_op jit(solution)/shard_map/mix/pallas_call | solution.py:333
  415.5 0.6 multiply_reduce_fusion
  416.1 289.0 %give_back.1.home_ref = f32[2,2,8,64,4096]{4,3,2,1,0:T(8,128)} custom-call(f32[2,64,64,1024]{3,2,1,0:T(8,128)} %get-tuple-element.4.rows_ref), custom_call_target="tpu_custom_call" | custom-call | tf_op jit(solution)/shard_map/give_back/pallas_call | solution.py:364
  705.1 37.9 %psum.7 = f32[]{:T(128)} all-reduce(f32[]{:T(128)} %multiply_reduce_fusion), channel_id=1, replica_groups=mesh['pairs'=8,'cols'=4] {'pairs','cols'}, use_global_device_ids=true, to_apply=%region_1.2 | all-reduce | flops 1 | bytes 8 | tf_op jit(solution)/shard_map/psum | solution.py:361
  743.7 18.5 %evolve.1 = f32[2,8,64,4096]{3,2,1,0:T(8,128)} custom-call(s32[1]{0:T(128)} %bitcast.offset_ref, f32[2,8,4096]{2,1,0:T(8,128)S(1)} %pad_maximum_fusion.1.one_ref, f32[2,64,4096]{2,1,0:T(8,128)S(1)} %pad_maximum_fusion.two_ref, f32[2,2,8,64,4096]{4,3,2,1,0:T(8,128)} %give_back.1.home_ref), custom_call_target="tpu_custom_call" | custom-call | tf_op jit(solution)/shard_map/evolve/pallas_call | solution.py:385
  (3 shorter events, 0.0 us)
Async XLA Ops:
  7.2 285.2 %all-gather.2.cloned.1.call-start = ((), (), s32[]{:S(2)}) async-start(), calls=%async_computation | async-start | bytes 2621440 | tf_op jit(solution)/shard_map/all_gather | solution.py:302
  9.3 276.7 %copy-start.1 = (f32[2]{0:T(128)S(1)}, f32[2]{0:T(128)}, u32[]{:S(2)}) copy-start(f32[2]{0:T(128)} %param.6) | copy-start | bytes 28
  9.3 277.3 %copy-start = (s32[4096]{0:T(1024)S(1)}, s32[4096]{0:T(1024)}, u32[]{:S(2)}) copy-start(s32[4096]{0:T(1024)} %param.7) | copy-start | bytes 49156
Sparse Core Ops, SparseCore 0:
  10.1 24.1 all-gather.1

commit v2 on v0

v2 whole, which is shorter than its diff:
```python
import functools

import jax
import jax.numpy as jnp
from jax import lax
from jax.experimental import pallas as pl
from jax.experimental.pallas import tpu as pltpu
from jax.sharding import PartitionSpec as P

THIRD = 64
MEMB = 128
WINDOW = 2
BAND = 8
LANES = 128
CHUNK = 256
MESH = pl.DeviceIdType.MESH


def band_count(group, p, local_one, levels):
    lower = lax.div(levels - 1 - p * local_one, BAND) + 1
    upper = levels // BAND - lax.div(levels + 1 - local_one - p * local_one, BAND)
    return jnp.where(group == 0, lower, upper)


def mix_kernel(
    count, groups, levels,
    state_ref, slab_ref, home_ref, moment_ref,
    rows, slabs, planes, factors, own_moment, pair_moments, col_moments,
    go_sem, come_sem, back_sem, home_sem, own_sem, own_home_sem,
    slab_send, slab_recv, slab_own, mp_send, mp_recv, mc_send, mc_recv,
):
    me = lax.axis_index("pairs")
    mine = lax.axis_index("cols")
    local_one, columns = state_ref.shape[1], state_ref.shape[3]
    half = count // 2
    width = columns // half
    chunk = min(CHUNK, width)
    chunks = width // chunk
    bands = levels // BAND
    depth = slab_ref.shape[1]
    group = lax.div(me, half)

    barrier = pltpu.get_barrier_semaphore()

    def greet_pair(k, carry):
        pl.semaphore_signal(
            barrier, inc=1, device_id=(lax.rem(me + k, count), mine), device_id_type=MESH
        )
        return carry

    def greet_col(k, carry):
        pl.semaphore_signal(
            barrier, inc=1, device_id=(me, lax.rem(mine + k, groups)), device_id_type=MESH
        )
        return carry

    lax.fori_loop(1, count, greet_pair, 0)
    lax.fori_loop(1, groups, greet_col, 0)
    pl.semaphore_wait(barrier, count + groups - 2)

    def at_home(ref, owner, c, n):
        first = lax.div(owner, half) * (levels - n * BAND)
        start = lax.rem(owner, half) * width + c * chunk
        return ref.at[
            :, :, pl.ds(pl.multiple_of(first, BAND), n * BAND),
            pl.ds(pl.multiple_of(start, LANES), chunk),
        ]

    def at_owner(owner, p, c, n):
        first = lax.div(owner, half) * (levels - n * BAND)
        return rows.at[
            :, pl.ds(p * local_one, local_one), pl.ds(pl.multiple_of(first, BAND), n * BAND),
            pl.ds(pl.multiple_of(c * chunk, LANES), chunk),
        ]

    def sized(owner, p, act):
        found = band_count(lax.div(owner, half), p, local_one, levels)
        for n in range(1, bands + 1):
            @pl.when(found == n)
            def _():
                act(n)

    def go(p, owner, c, n):
        return pltpu.make_async_remote_copy(
            src_ref=at_home(state_ref, owner, c, n),
            dst_ref=at_owner(owner, p, c, n),
            send_sem=go_sem.at[owner, c],
            recv_sem=come_sem.at[p, c],
            device_id=(owner, mine),
            device_id_type=MESH,
        )

    def back(owner, p, c, n):
        return pltpu.make_async_remote_copy(
            src_ref=at_owner(owner, p, c, n),
            dst_ref=at_home(home_ref.at[lax.div(owner, half)], owner, c, n),
            send_sem=back_sem.at[p, c],
            recv_sem=home_sem.at[owner, c],
            device_id=(p, mine),
            device_id_type=MESH,
        )

    def own_go(c, n):
        return pltpu.make_async_copy(
            at_home(state_ref, me, c, n), at_owner(me, me, c, n), own_sem.at[c]
        )

    def own_back(c, n):
        return pltpu.make_async_copy(
            at_owner(me, me, c, n), at_home(home_ref.at[group], me, c, n), own_home_sem.at[c]
        )

    def peers(act):
        def body(k, carry):
            act(lax.rem(me + k, count))
            return carry

        lax.fori_loop(1, count, body, 0)

    def col_peers(act):
        def body(k, carry):
            act(lax.rem(mine + k, groups))
            return carry

        lax.fori_loop(1, groups, body, 0)

    def slab_place(col):
        return slabs.at[:, pl.ds(pl.multiple_of(col * depth, BAND), depth), :]

    def slab(source, dest):
        return pltpu.make_async_remote_copy(
            src_ref=slab_ref,
            dst_ref=slab_place(source),
            send_sem=slab_send.at[dest],
            recv_sem=slab_recv.at[source],
            device_id=(me, dest),
            device_id_type=MESH,
        )

    slab_here = pltpu.make_async_copy(slab_ref, slab_place(mine), slab_own)
    col_peers(lambda dest: slab(mine, dest).start())
    slab_here.start()

    def send_chunk(c, carry):
        peers(lambda dest: sized(dest, me, lambda n: go(me, dest, c, n).start()))
        sized(me, me, lambda n: own_go(c, n).start())
        return carry

    lax.fori_loop(0, chunks, send_chunk, 0)

    col_peers(lambda source: slab(source, mine).wait_recv())
    slab_here.wait()

    def turn(i, carry):
        wide = jnp.concatenate(
            [slabs[i], jnp.zeros((LANES - levels, LANES), jnp.float32)], axis=0
        )
        planes[0, pl.ds(i, 2 * levels, stride=levels), :] = wide.T
        return carry

    lax.fori_loop(0, levels, turn, 0)

    def split(t, carry):
        start = pl.multiple_of((group * levels + t) * levels, BAND)
        whole = planes[0, pl.ds(start, levels), :][:, :levels]
        high = whole.astype(jnp.bfloat16)
        low = (whole - high.astype(jnp.float32)).astype(jnp.bfloat16)
        factors[t] = jnp.concatenate([high, high, low], axis=1)
        return carry

    lax.fori_loop(0, levels, split, 0)

    def clear(i, carry):
        start = pl.multiple_of(i * levels, BAND)
        for part in range(2):
            planes[part, pl.ds(start, levels), :] = jnp.zeros((levels, LANES), jnp.float32)
        return carry

    lax.fori_loop(0, 2 * levels, clear, 0)
    own_moment[...] = jnp.zeros_like(own_moment)
    row_ids = lax.broadcasted_iota(jnp.int32, (levels, 2 * LANES), 0)

    def both(act):
        @pl.when(group == 0)
        def _():
            def level(n1, carry):
                act(n1, pl.ds(n1 * (levels + 1), levels, stride=levels))
                return carry

            lax.fori_loop(0, levels, level, 0, unroll=2)

        @pl.when(group == 1)
        def _():
            def level(n1, carry):
                act(n1, pl.ds(n1 * levels + levels - 1, levels, stride=levels - 1))
                return carry

            lax.fori_loop(0, levels, level, 0, unroll=2)

    def mix_tile(start_column):
        lanes = pl.ds(pl.multiple_of(start_column, LANES), LANES)

        def put(n1, where):
            for part in range(2):
                planes[part, where, :] = rows[part, n1, :, lanes]

        def get(n1, where):
            for part in range(2):
                rows[part, n1, :, lanes] = planes[part, where, :]

        both(put)

        def sector(t, total):
            start = pl.multiple_of((group * levels + t) * levels, BAND)
            block = jnp.concatenate(
                [planes[0, pl.ds(start, levels), :], planes[1, pl.ds(start, levels), :]], axis=1
            )
            high = block.astype(jnp.bfloat16)
            low = (block - high.astype(jnp.float32)).astype(jnp.bfloat16)
            found = jnp.dot(
                factors[t],
                jnp.concatenate([high, low, high], axis=0),
                preferred_element_type=jnp.float32,
            )
            size = jnp.where(group == 0, t + 1, levels - 1 - t)
            first = jnp.where(group == 0, 0, t + 1)
            found = jnp.where(row_ids < size, found, 0.0)
            planes[0, pl.ds(start, levels), :] = found[:, :LANES]
            planes[1, pl.ds(start, levels), :] = found[:, LANES:]
            term = (row_ids + (first + 1)).astype(jnp.float32) * found * found
            for band in range(bands):
                total = total + term[band * BAND : (band + 1) * BAND]
            return total

        total = lax.fori_loop(
            0, levels, sector, jnp.zeros((BAND, 2 * LANES), jnp.float32), unroll=4
        )
        column = mine * columns + lax.rem(me, half) * width + start_column
        third = lax.div(column, MEMB * WINDOW).astype(jnp.float32)
        own_moment[...] += (third + 1.0) * (total[:, :LANES] + total[:, LANES:])
        both(get)

    def mix_chunk(c, carry):
        peers(lambda source: sized(me, source, lambda n: go(source, me, c, n).wait_recv()))
        sized(me, me, lambda n: own_go(c, n).wait())

        def tile(i, carry):
            mix_tile(c * chunk + i * LANES)
            return carry

        lax.fori_loop(0, chunk // LANES, tile, 0)
        peers(lambda p: sized(me, p, lambda n: back(me, p, c, n).start()))
        sized(me, me, lambda n: own_back(c, n).start())
        return carry

    lax.fori_loop(0, chunks, mix_chunk, 0)

    def moment_pair(source, dest):
        return pltpu.make_async_remote_copy(
            src_ref=own_moment, dst_ref=pair_moments.at[source],
            send_sem=mp_send.at[dest], recv_sem=mp_recv.at[source],
            device_id=(dest, mine), device_id_type=MESH,
        )

    def moment_col(source, dest):
        return pltpu.make_async_remote_copy(
            src_ref=moment_ref, dst_ref=col_moments.at[source],
            send_sem=mc_send.at[dest], recv_sem=mc_recv.at[source],
            device_id=(me, dest), device_id_type=MESH,
        )

    peers(lambda dest: moment_pair(me, dest).start())
    pair_moments[me] = own_moment[...]
    peers(lambda source: moment_pair(source, me).wait_recv())
    moment_ref[...] = jnp.sum(pair_moments[...], axis=0)
    col_peers(lambda dest: moment_col(mine, dest).start())
    col_moments[mine] = moment_ref[...]
    col_peers(lambda source: moment_col(source, mine).wait_recv())
    col_peers(lambda dest: moment_col(mine, dest).wait_send())
    moment_ref[...] = jnp.sum(col_moments[...], axis=0)

    peers(lambda dest: moment_pair(me, dest).wait_send())
    col_peers(lambda dest: slab(mine, dest).wait_send())

    def finish(c, carry):
        peers(lambda dest: sized(dest, me, lambda n: go(me, dest, c, n).wait_send()))
        peers(lambda p: sized(me, p, lambda n: back(me, p, c, n).wait_send()))
        peers(lambda owner: sized(owner, me, lambda n: back(owner, me, c, n).wait_recv()))
        sized(me, me, lambda n: own_back(c, n).wait())
        return carry

    lax.fori_loop(0, chunks, finish, 0)


def evolve_kernel(levels, offset_ref, one_ref, two_ref, home_ref, evolved_ref):
    offset = offset_ref[0]
    local_one = home_ref.shape[2]
    shape = home_ref.shape[3:]
    n2 = lax.broadcasted_iota(jnp.int32, shape, 0)
    cos_two, sin_two = two_ref[0], two_ref[1]
    for i in range(local_one):
        lower = n2 + (offset + i) < levels
        real = jnp.where(lower, home_ref[0, 0, i], home_ref[1, 0, i])
        imag = jnp.where(lower, home_ref[0, 1, i], home_ref[1, 1, i])
        cos_one, sin_one = one_ref[0, i : i + 1, :], one_ref[1, i : i + 1, :]
        cosine = cos_one * cos_two - sin_one * sin_two
        sine = sin_one * cos_two + cos_one * sin_two
        evolved_ref[0, i] = cosine * real - sine * imag
        evolved_ref[1, i] = sine * real + cosine * imag


def local(state, sector_mix, kerr_rates, column_load):
    count = lax.axis_size("pairs")
    groups = lax.axis_size("cols")
    me = lax.axis_index("pairs")
    _, local_one, levels, columns = state.shape
    half = count // 2
    width = columns // half
    chunks = width // min(CHUNK, width)
    f32 = jnp.float32
    anywhere = pl.BlockSpec(memory_space=pl.ANY)
    tile = (BAND, LANES)
    dma = pltpu.SemaphoreType.DMA

    slab = jnp.pad(
        jnp.transpose(sector_mix, (1, 2, 0)),
        ((0, 0), (0, 0), (0, 2 * levels - sector_mix.shape[0])),
    )
    home, moments = pl.pallas_call(
        functools.partial(mix_kernel, count, groups, levels),
        out_shape=(
            jax.ShapeDtypeStruct((2, 2, local_one, levels, columns), f32),
            jax.ShapeDtypeStruct(tile, f32),
        ),
        in_specs=[anywhere, anywhere],
        out_specs=(anywhere, pl.BlockSpec(memory_space=pltpu.VMEM)),
        scratch_shapes=[
            pltpu.VMEM((2, levels, levels, width), f32),
            pltpu.VMEM((levels, levels, 2 * levels), f32),
            pltpu.VMEM((2, 2 * levels * levels, LANES), f32),
            pltpu.VMEM((levels, levels, 3 * levels), jnp.bfloat16),
            pltpu.VMEM(tile, f32),
            pltpu.VMEM((count,) + tile, f32),
            pltpu.VMEM((groups,) + tile, f32),
            dma((count, chunks)), dma((count, chunks)),
            dma((count, chunks)), dma((count, chunks)),
            dma((chunks,)), dma((chunks,)),
            dma((groups,)), dma((groups,)), dma,
            dma((count,)), dma((count,)), dma((groups,)), dma((groups,)),
        ],
        compiler_params=pltpu.CompilerParams(
            collective_id=0, has_side_effects=True, vmem_limit_bytes=58 << 20
        ),
        name="mix",
    )(state, slab)
    moment = jnp.sum(moments) / float(levels * levels * columns * groups * levels * THIRD)

    loads = column_load.astype(f32)
    offset = me * local_one
    levels_one = (offset + jnp.arange(local_one)).astype(f32)
    levels_two = jnp.arange(levels).astype(f32)
    phase_one = (kerr_rates[0] * levels_one)[:, None] * loads[None, :]
    phase_two = (kerr_rates[1] * levels_two)[:, None] * loads[None, :]
    one = jnp.stack([jnp.cos(phase_one), jnp.sin(phase_one)])
    two = jnp.stack([jnp.cos(phase_two), jnp.sin(phase_two)])
    tile_columns = min(columns, 512)
    evolved = pl.pallas_call(
        functools.partial(evolve_kernel, levels),
        grid=(columns // tile_columns,),
        out_shape=jax.ShapeDtypeStruct((2, local_one, levels, columns), f32),
        in_specs=[
            pl.BlockSpec(memory_space=pltpu.SMEM),
            pl.BlockSpec((2, local_one, tile_columns), lambda c: (0, 0, c)),
            pl.BlockSpec((2, levels, tile_columns), lambda c: (0, 0, c)),
            pl.BlockSpec((2, 2, local_one, levels, tile_columns), lambda c: (0, 0, 0, 0, c)),
        ],
        out_specs=pl.BlockSpec((2, local_one, levels, tile_columns), lambda c: (0, 0, 0, c)),
        compiler_params=pltpu.CompilerParams(vmem_limit_bytes=48 << 20),
        name="evolve",
    )(offset.reshape(1).astype(jnp.int32), one, two, home)
    return (evolved, moment.reshape(1))


def solution(mesh):
    placed = (P(None, "pairs", None, "cols"), P(None, None, "cols"), P(), P("cols"))
    return jax.shard_map(
        local,
        mesh=mesh,
        in_specs=placed,
        out_specs=(P(None, "pairs", None, "cols"), P()),
        check_vma=False,
    )
```

time: 2120 us -> 596 us (0.28)
  waiting for transfers between devices: 1060 us -> 0 us
  local copies, waits for them, and re-layouts: 741 us -> 3.19 us
  Pallas kernels: 0 us -> 582 us
  other arithmetic: 154 us -> 7.72 us
  matrix products: 51.7 us -> 0 us
  starting transfers between devices: 45.5 us -> 0 us
  blocking collectives: 40.2 us -> 0 us
    all_to_all x2 -> x0, waiting for transfers between devices: 1040 us -> none  [the longest x1 717 us: local(): lax.all_to_all(leaving, 'pairs', split_axis=1, concat_axis=1, tiled=True)]
    gather x6 -> x0, local copies, waits for them, and re-layouts: 616 us -> none  [the longest x2 363 us: local(): jnp.take(flat_mix, jnp.maximum(my_mat, 0))]
    pallas_call x0 -> x2, Pallas kernels: none -> 582 us  [the longest x1 563 us: local(): pl.pallas_call(functools.partial(mix_kernel, count, groups, levels), out_...]
    select_n x6 -> x0, other arithmetic: 104 us -> none  [the longest x1 29.5 us: local(): jnp.take(arrived.reshape(2, pair_count * slot_count, item_count), my_layo...]
    reshape x2 -> x0, local copies, waits for them, and re-layouts: 58.5 us -> none  [the longest x1 55.3 us: local(): combined.reshape(2, groups * levels, item_count)]
    dot_general x1 -> x0, matrix products: 51.7 us -> none  [local(): jnp.einsum('gij,pgjc->pgic', blocks, gathered, precision=lax.Precision.HI...]
    all_to_all x2 -> x0, starting transfers between devices: 45.3 us -> none  [the longest x1 38.3 us: local(): lax.all_to_all(leaving, 'pairs', split_axis=1, concat_axis=1, tiled=True)]
    psum x1 -> x0, blocking collectives: 40.2 us -> none  [local(): summed = lax.psum(partial_term, ('pairs', 'cols'))]
  transfers between devices with their start and end apart: 3 -> 0, of which waited for: 3 -> 0; matrix products, arithmetic and copies ran while one was open for 18% -> 0% of each run, Pallas kernels for 0% -> 0%
where the time goes in v2:
time: 596 us; the launch traced here: 595 us
  Pallas kernels  582 us (98%)
  other arithmetic  7.72 us (1%)
    pallas_call x1, Pallas kernels, local(): pl.pallas_call(functools.partial(mix_kernel, count, groups, levels), out_...  563 us
    pallas_call x1, Pallas kernels, local(): pl.pallas_call(functools.partial(evolve_kernel, levels), grid=(columns //...  18.5 us

profile of v2, /device:TPU:9, one launch (start us, length us, event | category | flops | bytes accessed | tf_op | source)
XLA Modules:
  0.0 595.4 jit_solution(17982028629959822102)
XLA Ops:
  0.6 1.3 fusion
  1.9 0.6 convert_multiply_fusion
  2.6 0.7 convert_multiply_fusion.1
  3.3 0.7 convert_element_type.20
  4.0 0.5 multiply_cosine_fusion.1
  4.6 1.9 pad.4.slab_ref
  6.4 3.7 multiply_cosine_fusion
  10.1 0.2 pad_maximum_fusion.two_ref
  10.3 563.4 %mix.1 = (f32[2,2,8,64,4096]{4,3,2,1,0:T(8,128)}, f32[8,128]{1,0:T(8,128)}) custom-call(f32[2,8,64,4096]{3,2,1,0:T(8,128)} %state_ref.1, f32[64,16,128]{2,1,0:T(8,128)} %pad.4.slab_ref), custom_call_target="tpu_custom_call" | custom-call | tf_op jit(solution)/shard_map/mix/pallas_call | solution.py:329
  573.8 1.3 reduce_sum.9
  575.7 18.5 %evolve.1 = f32[2,8,64,4096]{3,2,1,0:T(8,128)} custom-call(s32[1]{0:T(128)} %bitcast.offset_ref, f32[2,8,4096]{2,1,0:T(8,128)S(1)} %pad_maximum_fusion.1.one_ref, f32[2,64,4096]{2,1,0:T(8,128)S(1)} %pad_maximum_fusion.two_ref, f32[2,2,8,64,4096]{4,3,2,1,0:T(8,128)} %get-tuple-element.4.home_ref), custom_call_target="tpu_custom_call" | custom-call | tf_op jit(solution)/shard_map/evolve/pallas_call | solution.py:367
  (1 shorter events, 0.0 us)

commit v3 on v2

--- a/solution.py
+++ b/solution.py
@@ -22,13 +22,26 @@
     return jnp.where(group == 0, lower, upper)
 
 
+def turned(tile, by):
+    return jnp.concatenate([tile[BAND - by :], tile[: BAND - by]], axis=0)
+
+
+def joined(take, k, group):
+    ids = lax.broadcasted_iota(jnp.int32, take(0).shape, 0)
+    kept, moved = take(k), turned(take(BAND - k), BAND - k)
+    return jnp.where((ids < BAND - k) == (group == 0), kept, moved)
+
+
 def mix_kernel(
     count, groups, levels,
-    state_ref, slab_ref, home_ref, moment_ref,
+    state_ref, slab_ref, home_ref, moment_ref, diag_ref,
     rows, slabs, planes, factors, own_moment, pair_moments, col_moments,
     go_sem, come_sem, back_sem, home_sem, own_sem, own_home_sem,
     slab_send, slab_recv, slab_own, mp_send, mp_recv, mc_send, mc_recv,
+    stage=None, tiles=None, packs=None, stage_sem=None, pack_go_sem=None, pack_come_sem=None,
+    pack_back_sem=None, pack_home_sem=None, pack_own_sem=None, pack_own_home_sem=None,
 ):
+    packed = stage is not None
     me = lax.axis_index("pairs")
     mine = lax.axis_index("cols")
     local_one, columns = state_ref.shape[1], state_ref.shape[3]
@@ -74,7 +87,7 @@
         ]
 
     def sized(owner, p, act):
-        found = band_count(lax.div(owner, half), p, local_one, levels)
+        found = band_count(lax.div(owner, half), p, local_one, levels) - int(packed)
         for n in range(1, bands + 1):
             @pl.when(found == n)
             def _():
@@ -110,6 +123,59 @@
             at_owner(me, me, c, n), at_home(home_ref.at[group], me, c, n), own_home_sem.at[c]
         )
 
+    def columns_of(owner, c):
+        start = lax.rem(owner, half) * width + c * chunk
+        return pl.ds(pl.multiple_of(start, LANES), chunk)
+
+    def pack_tiles(owner, act):
+        if not packed:
+            return
+        for which in range(2):
+            @pl.when(lax.div(owner, half) == which)
+            def _():
+                act(which)
+
+    def pack_at_owner(p, c, which):
+        return packs.at[
+            :, p, pl.ds(0, 5 - which), :, pl.ds(pl.multiple_of(c * chunk, LANES), chunk)
+        ]
+
+    def pack_at_home(owner, c, which):
+        return tiles.at[:, pl.ds(5 * which, 5 - which), :, columns_of(owner, c)]
+
+    def pack_result(owner, c, which):
+        return diag_ref.at[which, :, pl.ds(0, 5 - which), :, columns_of(owner, c)]
+
+    def pack_go(p, owner, c, which):
+        return pltpu.make_async_remote_copy(
+            src_ref=pack_at_home(owner, c, which),
+            dst_ref=pack_at_owner(p, c, which),
+            send_sem=pack_go_sem.at[owner, c],
+            recv_sem=pack_come_sem.at[p, c],
+            device_id=(owner, mine),
+            device_id_type=MESH,
+        )
+
+    def pack_back(owner, p, c, which):
+        return pltpu.make_async_remote_copy(
+            src_ref=pack_at_owner(p, c, which),
+            dst_ref=pack_result(owner, c, which),
+            send_sem=pack_back_sem.at[p, c],
+            recv_sem=pack_home_sem.at[owner, c],
+            device_id=(p, mine),
+            device_id_type=MESH,
+        )
+
+    def pack_own_go(c, which):
+        return pltpu.make_async_copy(
+            pack_at_home(me, c, which), pack_at_owner(me, c, which), pack_own_sem.at[c]
+        )
+
+    def pack_own_back(c, which):
+        return pltpu.make_async_copy(
+            pack_at_owner(me, c, which), pack_result(me, c, which), pack_own_home_sem.at[c]
+        )
+
     def peers(act):
         def body(k, carry):
             act(lax.rem(me + k, count))
@@ -141,9 +207,36 @@
     col_peers(lambda dest: slab(mine, dest).start())
     slab_here.start()
 
+    if packed:
+        meet = pl.ds(pl.multiple_of(levels - BAND - me * BAND, BAND), BAND)
+        staged = pltpu.make_async_copy(state_ref.at[:, :, meet, :], stage, stage_sem)
+        staged.start()
+        staged.wait()
+
+        def pack(c, carry):
+            lanes = pl.ds(pl.multiple_of(c * chunk, LANES), chunk)
+            for part in range(2):
+                def take(i):
+                    return stage[part, i, :, lanes]
+
+                tiles[part, 0, :, lanes] = take(0)
+                for k in range(1, 4):
+                    for which in range(2):
+                        tiles[part, 4 * which + k, :, lanes] = joined(take, k, which)
+                for which in range(2):
+                    tiles[part, 4 + 4 * which, :, lanes] = take(4)
+            return carry
+
+        lax.fori_loop(0, columns // chunk, pack, 0)
+
     def send_chunk(c, carry):
-        peers(lambda dest: sized(dest, me, lambda n: go(me, dest, c, n).start()))
+        def send(dest):
+            sized(dest, me, lambda n: go(me, dest, c, n).start())
+            pack_tiles(dest, lambda which: pack_go(me, dest, c, which).start())
+
+        peers(send)
         sized(me, me, lambda n: own_go(c, n).start())
+        pack_tiles(me, lambda which: pack_own_go(c, which).start())
         return carry
 
     lax.fori_loop(0, chunks, send_chunk, 0)
@@ -241,16 +334,58 @@
         both(get)
 
     def mix_chunk(c, carry):
-        peers(lambda source: sized(me, source, lambda n: go(source, me, c, n).wait_recv()))
+        def arrive(source):
+            sized(me, source, lambda n: go(source, me, c, n).wait_recv())
+            pack_tiles(me, lambda which: pack_go(source, me, c, which).wait_recv())
+
+        peers(arrive)
         sized(me, me, lambda n: own_go(c, n).wait())
+        pack_tiles(me, lambda which: pack_own_go(c, which).wait())
+        lanes = pl.ds(pl.multiple_of(c * chunk, LANES), chunk)
+
+        def place(p, i, part):
+            band = pl.ds(pl.multiple_of(levels - BAND - p * BAND, BAND), BAND)
+            return (part, p * BAND + i, band, lanes)
+
+        def unpack(p, carry):
+            for part in range(2):
+                rows[place(p, 0, part)] = packs[part, p, 0, :, lanes]
+                for k in range(1, 4):
+                    found = packs[part, p, k - group, :, lanes]
+                    rows[place(p, k, part)] = found
+                    rows[place(p, BAND - k, part)] = turned(found, k)
+                rows[place(p, 4, part)] = packs[part, p, 4 - group, :, lanes]
+            return carry
+
+        def repack(p, carry):
+            for part in range(2):
+                def take(i):
+                    return rows[place(p, i, part)]
+
+                packs[part, p, 0, :, lanes] = take(0)
+                for k in range(1, 4):
+                    packs[part, p, k - group, :, lanes] = joined(take, k, group)
+                packs[part, p, 4 - group, :, lanes] = take(4)
+            return carry
+
+        if packed:
+            lax.fori_loop(0, count, unpack, 0)
 
         def tile(i, carry):
             mix_tile(c * chunk + i * LANES)
             return carry
 
         lax.fori_loop(0, chunk // LANES, tile, 0)
-        peers(lambda p: sized(me, p, lambda n: back(me, p, c, n).start()))
+        if packed:
+            lax.fori_loop(0, count, repack, 0)
+
+        def leave(p):
+            sized(me, p, lambda n: back(me, p, c, n).start())
+            pack_tiles(me, lambda which: pack_back(me, p, c, which).start())
+
+        peers(leave)
         sized(me, me, lambda n: own_back(c, n).start())
+        pack_tiles(me, lambda which: pack_own_back(c, which).start())
         return carry
 
     lax.fori_loop(0, chunks, mix_chunk, 0)
@@ -287,12 +422,21 @@
         peers(lambda p: sized(me, p, lambda n: back(me, p, c, n).wait_send()))
         peers(lambda owner: sized(owner, me, lambda n: back(owner, me, c, n).wait_recv()))
         sized(me, me, lambda n: own_back(c, n).wait())
+
+        def finish_pack(peer):
+            pack_tiles(peer, lambda which: pack_go(me, peer, c, which).wait_send())
+            pack_tiles(me, lambda which: pack_back(me, peer, c, which).wait_send())
+            pack_tiles(peer, lambda which: pack_back(peer, me, c, which).wait_recv())
+
+        if packed:
+            peers(finish_pack)
+            pack_tiles(me, lambda which: pack_own_back(c, which).wait())
         return carry
 
     lax.fori_loop(0, chunks, finish, 0)
 
 
-def evolve_kernel(levels, offset_ref, one_ref, two_ref, home_ref, evolved_ref):
+def evolve_kernel(levels, packed, offset_ref, one_ref, two_ref, home_ref, diag_ref, evolved_ref):
     offset = offset_ref[0]
     local_one = home_ref.shape[2]
     shape = home_ref.shape[3:]
@@ -307,6 +451,30 @@
         sine = sin_one * cos_two + cos_one * sin_two
         evolved_ref[0, i] = cosine * real - sine * imag
         evolved_ref[1, i] = sine * real + cosine * imag
+    if not packed:
+        return
+    band = pl.ds(pl.multiple_of(levels - BAND - offset, BAND), BAND)
+    cos_two, sin_two = two_ref[0, band, :], two_ref[1, band, :]
+    ids = lax.broadcasted_iota(jnp.int32, cos_two.shape, 0)
+    for i in range(local_one):
+        k = min(i, BAND - i)
+        found = []
+        for part in range(2):
+            lower = diag_ref[0, part, k]
+            if i == 0:
+                found.append(lower)
+                continue
+            upper = diag_ref[1, part, k - 1]
+            if i <= 4:
+                found.append(jnp.where(ids < BAND - k, lower, upper))
+            else:
+                found.append(turned(jnp.where(ids < BAND - k, upper, lower), k))
+        real, imag = found
+        cos_one, sin_one = one_ref[0, i : i + 1, :], one_ref[1, i : i + 1, :]
+        cosine = cos_one * cos_two - sin_one * sin_two
+        sine = sin_one * cos_two + cos_one * sin_two
+        evolved_ref[0, i, band, :] = cosine * real - sine * imag
+        evolved_ref[1, i, band, :] = sine * real + cosine * imag
 
 
 def local(state, sector_mix, kerr_rates, column_load):
@@ -326,14 +494,25 @@
         jnp.transpose(sector_mix, (1, 2, 0)),
         ((0, 0), (0, 0), (0, 2 * levels - sector_mix.shape[0])),
     )
-    home, moments = pl.pallas_call(
+    packed = local_one == BAND
+    extra = [
+        pltpu.VMEM((2, local_one, BAND, columns), f32),
+        pltpu.VMEM((2, 9, BAND, columns), f32),
+        pltpu.VMEM((2, count, 5, BAND, width), f32),
+        dma,
+        dma((count, chunks)), dma((count, chunks)),
+        dma((count, chunks)), dma((count, chunks)),
+        dma((chunks,)), dma((chunks,)),
+    ]
+    home, moments, diag = pl.pallas_call(
         functools.partial(mix_kernel, count, groups, levels),
         out_shape=(
             jax.ShapeDtypeStruct((2, 2, local_one, levels, columns), f32),
             jax.ShapeDtypeStruct(tile, f32),
+            jax.ShapeDtypeStruct((2, 2, 5, BAND, columns), f32),
         ),
         in_specs=[anywhere, anywhere],
-        out_specs=(anywhere, pl.BlockSpec(memory_space=pltpu.VMEM)),
+        out_specs=(anywhere, pl.BlockSpec(memory_space=pltpu.VMEM), anywhere),
         scratch_shapes=[
             pltpu.VMEM((2, levels, levels, width), f32),
             pltpu.VMEM((levels, levels, 2 * levels), f32),
@@ -347,7 +526,7 @@
             dma((chunks,)), dma((chunks,)),
             dma((groups,)), dma((groups,)), dma,
             dma((count,)), dma((count,)), dma((groups,)), dma((groups,)),
-        ],
+        ] + (extra if packed else []),
         compiler_params=pltpu.CompilerParams(
             collective_id=0, has_side_effects=True, vmem_limit_bytes=58 << 20
         ),
@@ -365,7 +544,7 @@
     two = jnp.stack([jnp.cos(phase_two), jnp.sin(phase_two)])
     tile_columns = min(columns, 512)
     evolved = pl.pallas_call(
-        functools.partial(evolve_kernel, levels),
+        functools.partial(evolve_kernel, levels, packed),
         grid=(columns // tile_columns,),
         out_shape=jax.ShapeDtypeStruct((2, local_one, levels, columns), f32),
         in_specs=[
@@ -373,11 +552,12 @@
             pl.BlockSpec((2, local_one, tile_columns), lambda c: (0, 0, c)),
             pl.BlockSpec((2, levels, tile_columns), lambda c: (0, 0, c)),
             pl.BlockSpec((2, 2, local_one, levels, tile_columns), lambda c: (0, 0, 0, 0, c)),
+            pl.BlockSpec((2, 2, 5, BAND, tile_columns), lambda c: (0, 0, 0, 0, c)),
         ],
         out_specs=pl.BlockSpec((2, local_one, levels, tile_columns), lambda c: (0, 0, 0, c)),
         compiler_params=pltpu.CompilerParams(vmem_limit_bytes=48 << 20),
         name="evolve",
-    )(offset.reshape(1).astype(jnp.int32), one, two, home)
+    )(offset.reshape(1).astype(jnp.int32), one, two, home, diag)
     return (evolved, moment.reshape(1))
 
 

time: 596 us -> 512 us (0.86)
  Pallas kernels: 582 us -> 496 us
    pallas_call x1, Pallas kernels: 563 us -> 477 us  [local(): pl.pallas_call(functools.partial(mix_kernel, count, groups, levels), out_...]
where the time goes in v3:
time: 512 us; the launch traced here: 511 us
  Pallas kernels  496 us (97%)
  other arithmetic  7.71 us (2%)
    pallas_call x1, Pallas kernels, local(): pl.pallas_call(functools.partial(mix_kernel, count, groups, levels), out_...  477 us
    pallas_call x1, Pallas kernels, local(): pl.pallas_call(functools.partial(evolve_kernel, levels, packed), grid=(co...  18.8 us

profile of v3, /device:TPU:9, one launch (start us, length us, event | category | flops | bytes accessed | tf_op | source)
XLA Modules:
  0.0 511.4 jit_solution(17380859354265494340)
XLA Ops:
  0.6 1.3 fusion
  1.9 0.6 convert_multiply_fusion
  2.6 0.7 convert_multiply_fusion.1
  3.3 0.7 convert_element_type.20
  4.0 0.5 multiply_cosine_fusion.1
  4.6 1.9 pad.4.slab_ref
  6.4 3.7 multiply_cosine_fusion
  10.1 0.2 pad_maximum_fusion.two_ref
  10.3 477.5 %mix.1 = (f32[2,2,8,64,4096]{4,3,2,1,0:T(8,128)}, f32[8,128]{1,0:T(8,128)}, f32[2,2,5,8,4096]{4,3,2,1,0:T(8,128)}) custom-call(f32[2,8,64,4096]{3,2,1,0:T(8,128)} %state_ref.1, f32[64,16,128]{2,1,0:T(8,128)} %pad.4.slab_ref), custom_call_target="tpu_custom_call" | custom-call | tf_op jit(solution)/shard_map/mix/pallas_call | solution.py:507
  487.8 1.3 reduce_sum.9
  489.7 0.0 copy-start
  489.7 1.7 copy-done
  491.5 18.8 %evolve.1 = f32[2,8,64,4096]{3,2,1,0:T(8,128)} custom-call(s32[1]{0:T(128)} %bitcast.offset_ref, f32[2,8,4096]{2,1,0:T(8,128)S(1)} %pad_maximum_fusion.1.one_ref, f32[2,64,4096]{2,1,0:T(8,128)S(1)} %pad_maximum_fusion.two_ref, f32[2,2,8,64,4096]{4,3,2,1,0:T(8,128)} %get-tuple-element.5.home_ref, f32[2,2,5,8,4096]{4,3,2,1,0:T(8,128)S(1)} %copy-done), custom_call_target="tpu_custom_call" | custom-call | tf_op jit(solution)/shard_map/evolve/pallas_call | solution.py:546
  (1 shorter events, 0.0 us)
Async XLA Ops:
  489.7 1.7 copy-start

commit v4 on v3

--- a/solution.py
+++ b/solution.py
@@ -53,6 +53,10 @@
     depth = slab_ref.shape[1]
     group = lax.div(me, half)
 
+    if packed:
+        meet = pl.ds(pl.multiple_of(levels - BAND - me * BAND, BAND), BAND)
+        staged = pltpu.make_async_copy(state_ref.at[:, :, meet, :], stage, stage_sem)
+        staged.start()
     barrier = pltpu.get_barrier_semaphore()
 
     def greet_pair(k, carry):
@@ -93,6 +97,9 @@
             def _():
                 act(n)
 
+    def result_of(owner):
+        return home_ref.at[0 if packed else lax.div(owner, half)]
+
     def go(p, owner, c, n):
         return pltpu.make_async_remote_copy(
             src_ref=at_home(state_ref, owner, c, n),
@@ -106,7 +113,7 @@
     def back(owner, p, c, n):
         return pltpu.make_async_remote_copy(
             src_ref=at_owner(owner, p, c, n),
-            dst_ref=at_home(home_ref.at[lax.div(owner, half)], owner, c, n),
+            dst_ref=at_home(result_of(owner), owner, c, n),
             send_sem=back_sem.at[p, c],
             recv_sem=home_sem.at[owner, c],
             device_id=(p, mine),
@@ -120,7 +127,7 @@
 
     def own_back(c, n):
         return pltpu.make_async_copy(
-            at_owner(me, me, c, n), at_home(home_ref.at[group], me, c, n), own_home_sem.at[c]
+            at_owner(me, me, c, n), at_home(result_of(me), me, c, n), own_home_sem.at[c]
         )
 
     def columns_of(owner, c):
@@ -207,10 +214,19 @@
     col_peers(lambda dest: slab(mine, dest).start())
     slab_here.start()
 
+    def send_bands(c):
+        peers(lambda dest: sized(dest, me, lambda n: go(me, dest, c, n).start()))
+        sized(me, me, lambda n: own_go(c, n).start())
+
+    def send_packs(c):
+        if packed:
+            peers(
+                lambda dest: pack_tiles(dest, lambda which: pack_go(me, dest, c, which).start())
+            )
+            pack_tiles(me, lambda which: pack_own_go(c, which).start())
+
+    send_bands(0)
     if packed:
-        meet = pl.ds(pl.multiple_of(levels - BAND - me * BAND, BAND), BAND)
-        staged = pltpu.make_async_copy(state_ref.at[:, :, meet, :], stage, stage_sem)
-        staged.start()
         staged.wait()
 
         def pack(c, carry):
@@ -229,17 +245,14 @@
 
         lax.fori_loop(0, columns // chunk, pack, 0)
 
+    send_packs(0)
+
     def send_chunk(c, carry):
-        def send(dest):
-            sized(dest, me, lambda n: go(me, dest, c, n).start())
-            pack_tiles(dest, lambda which: pack_go(me, dest, c, which).start())
-
-        peers(send)
-        sized(me, me, lambda n: own_go(c, n).start())
-        pack_tiles(me, lambda which: pack_own_go(c, which).start())
-        return carry
-
-    lax.fori_loop(0, chunks, send_chunk, 0)
+        send_bands(c)
+        send_packs(c)
+        return carry
+
+    lax.fori_loop(1, chunks, send_chunk, 0)
 
     col_peers(lambda source: slab(source, mine).wait_recv())
     slab_here.wait()
@@ -443,9 +456,11 @@
     n2 = lax.broadcasted_iota(jnp.int32, shape, 0)
     cos_two, sin_two = two_ref[0], two_ref[1]
     for i in range(local_one):
-        lower = n2 + (offset + i) < levels
-        real = jnp.where(lower, home_ref[0, 0, i], home_ref[1, 0, i])
-        imag = jnp.where(lower, home_ref[0, 1, i], home_ref[1, 1, i])
+        real, imag = home_ref[0, 0, i], home_ref[0, 1, i]
+        if not packed:
+            lower = n2 + (offset + i) < levels
+            real = jnp.where(lower, real, home_ref[1, 0, i])
+            imag = jnp.where(lower, imag, home_ref[1, 1, i])
         cos_one, sin_one = one_ref[0, i : i + 1, :], one_ref[1, i : i + 1, :]
         cosine = cos_one * cos_two - sin_one * sin_two
         sine = sin_one * cos_two + cos_one * sin_two
@@ -495,6 +510,7 @@
         ((0, 0), (0, 0), (0, 2 * levels - sector_mix.shape[0])),
     )
     packed = local_one == BAND
+    results = 1 if packed else 2
     extra = [
         pltpu.VMEM((2, local_one, BAND, columns), f32),
         pltpu.VMEM((2, 9, BAND, columns), f32),
@@ -507,7 +523,7 @@
     home, moments, diag = pl.pallas_call(
         functools.partial(mix_kernel, count, groups, levels),
         out_shape=(
-            jax.ShapeDtypeStruct((2, 2, local_one, levels, columns), f32),
+            jax.ShapeDtypeStruct((results, 2, local_one, levels, columns), f32),
             jax.ShapeDtypeStruct(tile, f32),
             jax.ShapeDtypeStruct((2, 2, 5, BAND, columns), f32),
         ),
@@ -551,7 +567,7 @@
             pl.BlockSpec(memory_space=pltpu.SMEM),
             pl.BlockSpec((2, local_one, tile_columns), lambda c: (0, 0, c)),
             pl.BlockSpec((2, levels, tile_columns), lambda c: (0, 0, c)),
-            pl.BlockSpec((2, 2, local_one, levels, tile_columns), lambda c: (0, 0, 0, 0, c)),
+            pl.BlockSpec((results, 2, local_one, levels, tile_columns), lambda c: (0, 0, 0, 0, c)),
             pl.BlockSpec((2, 2, 5, BAND, tile_columns), lambda c: (0, 0, 0, 0, c)),
         ],
         out_specs=pl.BlockSpec((2, local_one, levels, tile_columns), lambda c: (0, 0, 0, c)),

time: 512 us -> 524 us (1.023)
  Pallas kernels: 496 us -> 508 us
    pallas_call x1, Pallas kernels: 477 us -> 493 us  [local(): pl.pallas_call(functools.partial(mix_kernel, count, groups, levels), out_...]
where the time goes in v4:
time: 524 us; the launch traced here: 523 us
  Pallas kernels  508 us (97%)
  other arithmetic  7.74 us (1%)
    pallas_call x1, Pallas kernels, local(): pl.pallas_call(functools.partial(mix_kernel, count, groups, levels), out_...  493 us
    pallas_call x1, Pallas kernels, local(): pl.pallas_call(functools.partial(evolve_kernel, levels, packed), grid=(co...  15.2 us

profile of v4, /device:TPU:9, one launch (start us, length us, event | category | flops | bytes accessed | tf_op | source)
XLA Modules:
  0.0 523.3 jit_solution(17607003184230413302)
XLA Ops:
  0.6 1.3 fusion
  1.9 0.6 convert_multiply_fusion
  2.6 0.7 convert_multiply_fusion.1
  3.3 0.7 convert_element_type.20
  4.0 0.5 multiply_cosine_fusion.1
  4.6 1.9 pad.4.slab_ref
  6.4 3.7 multiply_cosine_fusion
  10.1 0.2 pad_maximum_fusion.two_ref
  10.3 493.0 %mix.1 = (f32[1,2,8,64,4096]{4,3,2,1,0:T(8,128)}, f32[8,128]{1,0:T(8,128)}, f32[2,2,5,8,4096]{4,3,2,1,0:T(8,128)}) custom-call(f32[2,8,64,4096]{3,2,1,0:T(8,128)} %state_ref.1, f32[64,16,128]{2,1,0:T(8,128)} %pad.4.slab_ref), custom_call_target="tpu_custom_call" | custom-call | tf_op jit(solution)/shard_map/mix/pallas_call | solution.py:523
  503.3 1.3 reduce_sum.9
  505.3 0.0 copy-start
  505.3 1.7 copy-done
  507.0 15.2 %evolve.1 = f32[2,8,64,4096]{3,2,1,0:T(8,128)} custom-call(s32[1]{0:T(128)} %bitcast.offset_ref, f32[2,8,4096]{2,1,0:T(8,128)S(1)} %pad_maximum_fusion.1.one_ref, f32[2,64,4096]{2,1,0:T(8,128)S(1)} %pad_maximum_fusion.two_ref, f32[1,2,8,64,4096]{4,3,2,1,0:T(8,128)} %get-tuple-element.5.home_ref, f32[2,2,5,8,4096]{4,3,2,1,0:T(8,128)S(1)} %copy-done), custom_call_target="tpu_custom_call" | custom-call | tf_op jit(solution)/shard_map/evolve/pallas_call | solution.py:562
  (1 shorter events, 0.0 us)
Async XLA Ops:
  505.3 1.7 copy-start

commit v5 on v4

--- a/solution.py
+++ b/solution.py
@@ -12,7 +12,7 @@
 WINDOW = 2
 BAND = 8
 LANES = 128
-CHUNK = 256
+CHUNK = 128
 MESH = pl.DeviceIdType.MESH
 
 
@@ -214,18 +214,6 @@
     col_peers(lambda dest: slab(mine, dest).start())
     slab_here.start()
 
-    def send_bands(c):
-        peers(lambda dest: sized(dest, me, lambda n: go(me, dest, c, n).start()))
-        sized(me, me, lambda n: own_go(c, n).start())
-
-    def send_packs(c):
-        if packed:
-            peers(
-                lambda dest: pack_tiles(dest, lambda which: pack_go(me, dest, c, which).start())
-            )
-            pack_tiles(me, lambda which: pack_own_go(c, which).start())
-
-    send_bands(0)
     if packed:
         staged.wait()
 
@@ -245,14 +233,17 @@
 
         lax.fori_loop(0, columns // chunk, pack, 0)
 
-    send_packs(0)
-
     def send_chunk(c, carry):
-        send_bands(c)
-        send_packs(c)
-        return carry
-
-    lax.fori_loop(1, chunks, send_chunk, 0)
+        def send(dest):
+            sized(dest, me, lambda n: go(me, dest, c, n).start())
+            pack_tiles(dest, lambda which: pack_go(me, dest, c, which).start())
+
+        peers(send)
+        sized(me, me, lambda n: own_go(c, n).start())
+        pack_tiles(me, lambda which: pack_own_go(c, which).start())
+        return carry
+
+    lax.fori_loop(0, chunks, send_chunk, 0)
 
     col_peers(lambda source: slab(source, mine).wait_recv())
     slab_here.wait()

time: 524 us -> 506 us (0.966)
  Pallas kernels: 508 us -> 488 us
    pallas_call x1, Pallas kernels: 493 us -> 473 us  [local(): pl.pallas_call(functools.partial(mix_kernel, count, groups, levels), out_...]
where the time goes in v5:
time: 506 us; the launch traced here: 503 us
  Pallas kernels  488 us (96%)
  other arithmetic  7.74 us (2%)
    pallas_call x1, Pallas kernels, local(): pl.pallas_call(functools.partial(mix_kernel, count, groups, levels), out_...  473 us
    pallas_call x1, Pallas kernels, local(): pl.pallas_call(functools.partial(evolve_kernel, levels, packed), grid=(co...  15.2 us

profile of v5, /device:TPU:9, one launch (start us, length us, event | category | flops | bytes accessed | tf_op | source)
XLA Modules:
  0.0 503.3 jit_solution(14584462011657487210)
XLA Ops:
  0.6 1.3 fusion
  1.9 0.6 convert_multiply_fusion
  2.6 0.7 convert_multiply_fusion.1
  3.3 0.7 convert_element_type.20
  4.0 0.5 multiply_cosine_fusion.1
  4.6 1.9 pad.4.slab_ref
  6.4 3.7 multiply_cosine_fusion
  10.1 0.2 pad_maximum_fusion.two_ref
  10.3 473.0 %mix.1 = (f32[1,2,8,64,4096]{4,3,2,1,0:T(8,128)}, f32[8,128]{1,0:T(8,128)}, f32[2,2,5,8,4096]{4,3,2,1,0:T(8,128)}) custom-call(f32[2,8,64,4096]{3,2,1,0:T(8,128)} %state_ref.1, f32[64,16,128]{2,1,0:T(8,128)} %pad.4.slab_ref), custom_call_target="tpu_custom_call" | custom-call | tf_op jit(solution)/shard_map/mix/pallas_call | solution.py:514
  483.3 1.3 reduce_sum.9
  485.2 0.0 copy-start
  485.2 1.7 copy-done
  487.0 15.2 %evolve.1 = f32[2,8,64,4096]{3,2,1,0:T(8,128)} custom-call(s32[1]{0:T(128)} %bitcast.offset_ref, f32[2,8,4096]{2,1,0:T(8,128)S(1)} %pad_maximum_fusion.1.one_ref, f32[2,64,4096]{2,1,0:T(8,128)S(1)} %pad_maximum_fusion.two_ref, f32[1,2,8,64,4096]{4,3,2,1,0:T(8,128)} %get-tuple-element.5.home_ref, f32[2,2,5,8,4096]{4,3,2,1,0:T(8,128)S(1)} %copy-done), custom_call_target="tpu_custom_call" | custom-call | tf_op jit(solution)/shard_map/evolve/pallas_call | solution.py:553
  (1 shorter events, 0.0 us)
Async XLA Ops:
  485.2 1.7 copy-start

commit v6 on v5

--- a/solution.py
+++ b/solution.py
@@ -12,7 +12,7 @@
 WINDOW = 2
 BAND = 8
 LANES = 128
-CHUNK = 128
+CHUNK = 256
 MESH = pl.DeviceIdType.MESH
 
 

time: 506 us -> 504 us (level)
  no operation moved by 1% of the time
where the time goes in v6:
time: 504 us; the launch traced here: 503 us
  Pallas kernels  488 us (97%)
  other arithmetic  7.74 us (2%)
    pallas_call x1, Pallas kernels, local(): pl.pallas_call(functools.partial(mix_kernel, count, groups, levels), out_...  473 us
    pallas_call x1, Pallas kernels, local(): pl.pallas_call(functools.partial(evolve_kernel, levels, packed), grid=(co...  15.2 us

profile of v6, /device:TPU:9, one launch (start us, length us, event | category | flops | bytes accessed | tf_op | source)
XLA Modules:
  0.0 503.3 jit_solution(17322330671728955026)
XLA Ops:
  0.6 1.3 fusion
  1.9 0.6 convert_multiply_fusion
  2.6 0.7 convert_multiply_fusion.1
  3.3 0.7 convert_element_type.20
  4.0 0.5 multiply_cosine_fusion.1
  4.6 1.9 pad.4.slab_ref
  6.4 3.7 multiply_cosine_fusion
  10.1 0.2 pad_maximum_fusion.two_ref
  10.3 472.9 %mix.1 = (f32[1,2,8,64,4096]{4,3,2,1,0:T(8,128)}, f32[8,128]{1,0:T(8,128)}, f32[2,2,5,8,4096]{4,3,2,1,0:T(8,128)}) custom-call(f32[2,8,64,4096]{3,2,1,0:T(8,128)} %state_ref.1, f32[64,16,128]{2,1,0:T(8,128)} %pad.4.slab_ref), custom_call_target="tpu_custom_call" | custom-call | tf_op jit(solution)/shard_map/mix/pallas_call | solution.py:514
  483.2 1.3 reduce_sum.9
  485.2 0.0 copy-start
  485.2 1.7 copy-done
  486.9 15.2 %evolve.1 = f32[2,8,64,4096]{3,2,1,0:T(8,128)} custom-call(s32[1]{0:T(128)} %bitcast.offset_ref, f32[2,8,4096]{2,1,0:T(8,128)S(1)} %pad_maximum_fusion.1.one_ref, f32[2,64,4096]{2,1,0:T(8,128)S(1)} %pad_maximum_fusion.two_ref, f32[1,2,8,64,4096]{4,3,2,1,0:T(8,128)} %get-tuple-element.5.home_ref, f32[2,2,5,8,4096]{4,3,2,1,0:T(8,128)S(1)} %copy-done), custom_call_target="tpu_custom_call" | custom-call | tf_op jit(solution)/shard_map/evolve/pallas_call | solution.py:553
  (1 shorter events, 0.0 us)
Async XLA Ops:
  485.2 1.7 copy-start
